TPU v7x, 512 devices: a whole 4x8x8 slice. The times are simulated.
512 devices in a mesh: dp: 64 (over y, z), mp: 8 (over x, core).
Axes of the slice: x: 4, y: 8, z: 8, core: 2. Of those that a mesh axis runs over, the one named last changes fastest.
Arguments:
- tokens: bfloat16 [16384, 5376], P('dp', 'mp'), may hold values from -32 to 32
- factor_old: float32 [1344, 5376], P('dp', 'mp'), may hold values from -0.15 to 2.1
- basis: float32 [5376, 1344], P('mp'), may hold values from -0.15625 to 0.15625
Outputs:
- factor_new: float32 [1344, 5376], P('dp', 'mp')
- rotated: float32 [1344, 5376], P('dp', 'mp')
All inputs are finite; a program needn't handle non-finite values.
Results may differ from a plain program's by a relative error of at most 0.0003.
Values may be sent and summed in bfloat16 or wider, within the bound.
A program may use at most 64 MiB of HBM per device.

v0:
```python
import jax
import jax.numpy as jnp
from jax import lax
from jax.sharding import PartitionSpec as P

decay_rate = 0.95


def partner_2(block, axis, bit):
    count = lax.axis_size(axis)
    route = []
    for low in range(count):
        high = low | 1 << bit
        if high != low and high < count:
            route += [(low, high), (high, low)]
    return lax.ppermute(block, axis, route)


def token_products(left_cols, right_cols):
    return lax.dot_general(
        left_cols, right_cols, (((0,), (0,)), ((), ())), preferred_element_type=jnp.float32
    )


def shards(tokens, factor_old, basis):
    dp_count = lax.axis_size("dp")
    tok_rows, features = tokens.shape
    scale_new = (1.0 - decay_rate) / (tok_rows * dp_count)
    half_bit = lax.axis_index("mp") % 2
    partner = partner_2(tokens, "mp", 0)
    first_half = jnp.where(half_bit == 0, tokens, partner)
    second_half = jnp.where(half_bit == 0, partner, tokens)
    block_cols = jnp.concatenate([first_half, second_half], axis=1)
    gram = lax.psum_scatter(
        token_products(block_cols, tokens), "dp", scatter_dimension=0, tiled=True
    )
    factor_new = decay_rate * factor_old + scale_new * gram
    partial_sum = jnp.dot(factor_new, basis, precision=lax.Precision.HIGHEST)
    mine_part = lax.dynamic_slice_in_dim(partial_sum, half_bit * features, features, 1)
    other_part = lax.dynamic_slice_in_dim(partial_sum, (1 - half_bit) * features, features, 1)
    mine_part, other_part = (mine_part, other_part)
    rotated = mine_part + partner_2(other_part, "mp", 0)
    return (factor_new, rotated)


def solution(mesh):
    return jax.shard_map(
        shards,
        mesh=mesh,
        in_specs=(P("dp", "mp"), P("dp", "mp"), P("mp", None)),
        out_specs=(P("dp", "mp"), P("dp", "mp")),
        check_vma=False,
    )
```

profile of v0, /device:TPU:1, one launch (start us, length us, event | category | flops | bytes accessed | tf_op | source)
XLA Modules:
  0.0 207.6 jit_solution(13556498893569672233)
XLA Ops:
  7.2 0.0 all-reduce.3.cloned.1.call-start
  7.2 8.8 %collective-permute-start = (bf16[256,672]{0,1:T(8,128)(2,1)}, bf16[256,672]{0,1:T(8,128)(2,1)S(1)}, u32[]{:S(2)}, u32[]{:S(2)}) collective-permute-start(bf16[256,672]{0,1:T(8,128)(2,1)} %param.3), channel_id=1, source_target_pairs={{0,1},{1,0},{2,3},{3,2},{4,5},{5,4},{6,7},{7,6},{8,9},{9,8},{10,11... | collective-permute-start | bytes 1032200 | tf_op jit(solution)/shard_map/ppermute | solution.py:16
  16.0 1.5 collective-permute-done
  17.5 1.0 broadcast_select_fusion.1
  18.5 0.0 copy-start.1
  18.5 3.7 %fusion = f32[1344,672]{1,0:T(8,128)} fusion(bf16[256,672]{0,1:T(8,128)(2,1)} %param.3, bf16[256,672]{0,1:T(8,128)(2,1)S(1)} %get-tuple-element.3, bf16[256,672]{0,1:T(8,128)(2,1)S(1)} %get-tuple-element.2), kind=kOutput, calls=%fused_computation | convolution fusion | flops 463798272 | bytes 4644864 | tf_op jit(solution)/shard_map/dot_general | solution.py:20
  22.2 0.0 all-reduce.3.cloned.1.call-update
  22.2 1.3 dynamic-slice
  24.2 163.9 %all-reduce.3.cloned.1.call-done = f32[1344,672]{1,0:T(8,128)} async-done(((f32[1344,672]{1,0:T(8,128)}), f32[1344,672]{1,0:T(8,128)}) %all-reduce.3.cloned.1.call-update) | async-done | bytes 3612688
  188.1 0.0 copy-done.1
  188.1 0.9 fusion.4
  189.0 0.0 copy-start
  189.0 4.0 %fusion.6 = f32[21,1344]{1,0:T(8,128)S(1)} fusion(f32[21,672]{1,0:T(8,128)S(1)} %fusion.4, f32[672,1344]{1,0:T(8,128)} %param.5), kind=kOutput, calls=%fused_computation.11 | convolution fusion | flops 227598336 | bytes 3782016 | tf_op jit(solution)/shard_map/dot_general | solution.py:38
  193.0 0.1 constant_dynamic-slice_fusion
  193.1 6.0 %collective-permute-start.1 = (f32[21,672]{1,0:T(8,128)S(1)}, f32[21,672]{1,0:T(8,128)S(1)}, u32[]{:S(2)}, u32[]{:S(2)}) collective-permute-start(f32[21,672]{1,0:T(8,128)S(1)} %constant_dynamic-slice_fusion), channel_id=1, source_target_pairs={{0,1},{1,0},{2,3},{3,2},{4,5},{5,4},{6,7},{7,6},{8,9},{9,8},{10,11... | collective-permute-start | bytes 169352 | tf_op jit(solution)/shard_map/ppermute | solution.py:16
  199.1 0.9 collective-permute-done.1
  200.0 0.7 dynamic-slice_add_fusion
  200.7 0.0 copy-done
Async XLA Ops:
  7.2 180.9 %all-reduce.3.cloned.1.call-start = ((), (), s32[]{:S(2)}) async-start(), calls=%async_computation | async-start | bytes 8257536
  7.2 10.3 %collective-permute-start = (bf16[256,672]{0,1:T(8,128)(2,1)}, bf16[256,672]{0,1:T(8,128)(2,1)S(1)}, u32[]{:S(2)}, u32[]{:S(2)}) collective-permute-start(bf16[256,672]{0,1:T(8,128)(2,1)} %param.3), channel_id=1, source_target_pairs={{0,1},{1,0},{2,3},{3,2},{4,5},{5,4},{6,7},{7,6},{8,9},{9,8},{10,11... | collective-permute-start | bytes 1032200 | tf_op jit(solution)/shard_map/ppermute | solution.py:16
  18.5 169.6 %copy-start.1 = (f32[21,672]{1,0:T(8,128)S(1)}, f32[21,672]{1,0:T(8,128)}, u32[]{:S(2)}) copy-start(f32[21,672]{1,0:T(8,128)} %param.4) | copy-start | bytes 169348
  189.0 11.8 %copy-start = (f32[21,672]{1,0:T(8,128)}, f32[21,672]{1,0:T(8,128)S(1)}, u32[]{:S(2)}) copy-start(f32[21,672]{1,0:T(8,128)S(1)} %fusion.4) | copy-start | bytes 169348
  193.1 6.9 %collective-permute-start.1 = (f32[21,672]{1,0:T(8,128)S(1)}, f32[21,672]{1,0:T(8,128)S(1)}, u32[]{:S(2)}, u32[]{:S(2)}) collective-permute-start(f32[21,672]{1,0:T(8,128)S(1)} %constant_dynamic-slice_fusion), channel_id=1, source_target_pairs={{0,1},{1,0},{2,3},{3,2},{4,5},{5,4},{6,7},{7,6},{8,9},{9,8},{10,11... | collective-permute-start | bytes 169352 | tf_op jit(solution)/shard_map/ppermute | solution.py:16
Sparse Core Ops, SparseCore 0:
  22.4 165.6 all-reduce.2
where the time goes:
time: 208 us
  waiting for transfers between devices  166 us (80%)
  starting transfers between devices  14.8 us (7%)
  between operations  14.8 us (7%)
  matrix products  7.72 us (4%)
  other arithmetic  2.66 us (1%)
    unnamed x2, waiting for transfers between devices  164 us
    ppermute x2, starting transfers between devices, partner_2(): return lax.ppermute(block, axis, route)  14.8 us
  transfers between devices with their start and end apart: 3, of which 3 were waited for; matrix products, arithmetic and copies ran while one was open for 1% of the time, Pallas kernels for 0%

commit v1 on v0

v1 whole, which is shorter than its diff:
```python
import jax
import jax.numpy as jnp
from jax import lax
from jax.experimental import pallas as pl
from jax.experimental.pallas import tpu as pltpu
from jax.sharding import PartitionSpec as P

decay_rate = 0.95

MESH = pl.DeviceIdType.MESH
SIDE = 8
ROWS = 21
CHUNK = SIDE * ROWS
PAD = 176
HALF = 672
PIECES = 3
WIDE = 256
WIDTHS = (256, 256, 160)
RIGHT, LEFT = 0, 1
FIRST = (((0, 256), (0, 128), None), (None, (128, 256), (0, 256)))
ORDER = ((2, 0, 1), (0, 2, 1))
OFFSETS = (4, 3, -3, 2, -2, 1, -1)


def encode(value):
    return ((value * jnp.abs(value)) * (value * value)).astype(jnp.bfloat16)


def decode(code):
    code = code.astype(jnp.float32)
    root = lax.rsqrt(lax.rsqrt(jnp.abs(code)))
    return jnp.where(code < 0.0, -root, root)


def kernel(
    scale_new, tok, old, bas, f_out, r_out,
    own_x, par_x, gram, sums, sent, got, flat, codes, far, fac,
    base, base_hi, base_lo, prod, prod_got,
    load_sem, par_sem, s_send, s_recv, t_send, t_recv, p_send, p_recv, ready,
):
    dp, mp = lax.axis_index("dp"), lax.axis_index("mp")
    y, z, core = dp // SIDE, dp % SIDE, mp % 2
    not_core = 1 - core
    here = not_core * y + core * z
    across = core * y + not_core * z

    def along(step):
        to_y = (y + not_core * step + SIDE) % SIDE
        to_z = (z + core * step + SIDE) % SIDE
        return {"dp": to_y * SIDE + to_z, "mp": mp}

    def cross(step):
        to_y = (y + core * step + SIDE) % SIDE
        to_z = (z + not_core * step + SIDE) % SIDE
        return {"dp": to_y * SIDE + to_z, "mp": mp}

    partner = {"dp": dp, "mp": mp + 1 - 2 * core}

    load_x = pltpu.make_async_copy(tok, own_x, load_sem.at[0])
    load_b = pltpu.make_async_copy(bas, base, load_sem.at[1])
    load_f = pltpu.make_async_copy(old, fac, load_sem.at[2])
    barrier = pltpu.get_barrier_semaphore()
    for device in (partner, along(1), along(-1), cross(1), cross(-1)):
        pl.semaphore_signal(barrier, inc=1, device_id=device, device_id_type=MESH)
    load_x.start()
    load_b.start()
    load_f.start()
    pl.semaphore_wait(barrier, 5)
    give_x = pltpu.make_async_remote_copy(
        src_ref=tok, dst_ref=par_x, send_sem=par_sem.at[0], recv_sem=par_sem.at[1],
        device_id=partner, device_id_type=MESH,
    )
    give_x.start()

    def announce(number):
        for device in (cross(1), cross(-1)):
            pl.semaphore_signal(
                ready.at[number], inc=1, device_id=device, device_id_type=MESH
            )

    announce(0)
    load_x.wait()
    give_x.wait()

    row = lax.broadcasted_iota(jnp.int32, (PAD, 1), 0)
    group = (row * 3121) >> 16
    col_id = lax.broadcasted_iota(jnp.int32, (PAD, HALF), 1)

    def products(slot, position):
        in_y = CHUNK * position + row
        in_z = ROWS * position + CHUNK * group + (row - ROWS * group)
        feature = not_core * in_y + core * in_z
        feature = jnp.where(row < CHUNK, feature, -2 * HALF)
        picked = jnp.zeros((PAD, own_x.shape[0]), jnp.float32)
        for block, first in ((own_x, HALF * core), (par_x, HALF * not_core)):
            pick = jnp.where(col_id == feature - first, 1.0, 0.0).astype(jnp.bfloat16)
            picked += lax.dot_general(
                pick, block[...], (((1,), (1,)), ((), ())),
                preferred_element_type=jnp.float32,
            )
        left = picked.astype(jnp.bfloat16)
        for piece, width in enumerate(WIDTHS):
            gram[slot, piece, :, 0:width] = jnp.dot(
                left, own_x[:, WIDE * piece:WIDE * piece + width],
                preferred_element_type=jnp.float32,
            )

    def slot_of(way, step):
        return 0 if step == 0 else 2 * step - 1 + way

    def hop(way, step, piece):
        lanes = FIRST[way][piece] if step == 0 else (0, WIDE)
        here_at = (way, step, piece, slice(None), slice(*lanes))
        return pltpu.make_async_remote_copy(
            src_ref=sent.at[here_at], dst_ref=got.at[here_at],
            send_sem=s_send.at[way, step, piece], recv_sem=s_recv.at[way, step, piece],
            device_id=along(1 if way == RIGHT else -1), device_id_type=MESH,
        )

    def put(way, step, piece):
        arrived = FIRST[way][piece] if step == 1 else (0, WIDTHS[piece])
        if step == 0:
            lo, hi = FIRST[way][piece]
            hi = min(hi, WIDTHS[piece])
            sent[way, step, piece, :, lo:hi] = encode(gram[0, piece, :, lo:hi])
        else:
            slot = slot_of(way, step)
            if arrived is None:
                arrived = (0, 0)
            lo, hi = arrived
            hi = min(hi, WIDTHS[piece])
            if hi > lo:
                hop(way, step - 1, piece).wait_recv()
                total = gram[slot, piece, :, lo:hi] + decode(got[way, step - 1, piece, :, lo:hi])
                sent[way, step, piece, :, lo:hi] = encode(total)
            for a, b in ((0, lo), (hi, WIDTHS[piece])):
                if b > a:
                    sent[way, step, piece, :, a:b] = encode(gram[slot, piece, :, a:b])
        hop(way, step, piece).start()

    products(0, (here + 4) % SIDE)
    put(RIGHT, 0, 0)
    put(LEFT, 0, 2)
    put(RIGHT, 0, 1)
    put(LEFT, 0, 1)
    products(1, (here + 3) % SIDE)
    put(RIGHT, 1, ORDER[RIGHT][0])
    products(2, (here + 5) % SIDE)
    put(LEFT, 1, ORDER[LEFT][0])
    for place in (1, 2):
        put(RIGHT, 1, ORDER[RIGHT][place])
        put(LEFT, 1, ORDER[LEFT][place])
    pl.semaphore_wait(ready.at[0], 2)
    announce(1)
    products(3, (here + 2) % SIDE)
    products(4, (here + 6) % SIDE)
    for place in range(PIECES):
        put(RIGHT, 2, ORDER[RIGHT][place])
        put(LEFT, 2, ORDER[LEFT][place])
    pl.semaphore_wait(ready.at[1], 2)
    announce(2)
    products(5, (here + 1) % SIDE)
    products(6, (here + 7) % SIDE)
    for place in range(PIECES):
        put(RIGHT, 3, ORDER[RIGHT][place])
        put(LEFT, 3, ORDER[LEFT][place])
    products(7, here)
    load_b.wait()

    @pl.loop(0, HALF // 96)
    def _(part):
        at = pl.ds(pl.multiple_of(part * 96, 96), 96)
        for half in range(2):
            value = base[at, HALF * half:HALF * (half + 1)]
            high = value.astype(jnp.bfloat16)
            base_hi[half, at, :] = high
            base_lo[half, at, :] = (value - high.astype(jnp.float32)).astype(jnp.bfloat16)

    pl.semaphore_wait(ready.at[2], 2)

    def over(number, piece):
        to = (across + OFFSETS[number] + SIDE) % SIDE
        return pltpu.make_async_remote_copy(
            src_ref=codes.at[to, pl.ds(48 * piece, 48)],
            dst_ref=far.at[number, pl.ds(48 * piece, 48)],
            send_sem=t_send.at[number, piece], recv_sem=t_recv.at[number, piece],
            device_id=cross(OFFSETS[number]), device_id_type=MESH,
        )

    for piece in (0, 2, 1):
        width = WIDTHS[piece]
        hop(RIGHT, 3, piece).wait_recv()
        hop(LEFT, 3, piece).wait_recv()
        sums[piece, :, 0:width] = (
            gram[7, piece, :, 0:width]
            + decode(got[RIGHT, 3, piece, :, 0:width])
            + decode(got[LEFT, 3, piece, :, 0:width])
        )
        for to in range(SIDE):
            both = jnp.concatenate(
                [sums[piece, ROWS * to:ROWS * to + 24, 128 * t:128 * t + 128] for t in range(2)], 0
            )
            flat[to, 48 * piece:48 * piece + 48, :] = both
            codes[to, 48 * piece:48 * piece + 48, :] = encode(both)
        for number in range(len(OFFSETS)):
            over(number, piece).start()

    load_f.wait()
    for piece in (0, 2, 1):
        total = flat[across, 48 * piece:48 * piece + 48, :]
        for number in range(len(OFFSETS)):
            over(number, piece).wait_recv()
            total += decode(far[number, 48 * piece:48 * piece + 48, :])
        for t in range(2):
            lo = WIDE * piece + 128 * t
            hi = min(lo + 128, HALF)
            part = total[24 * t:24 * t + ROWS, 0:hi - lo]
            f_out[:, lo:hi] = decay_rate * fac[:, lo:hi] + scale_new * part

    value = f_out[...]
    value = jnp.concatenate([value, jnp.zeros((32 - ROWS, HALF), jnp.float32)], 0)
    high = value.astype(jnp.bfloat16)
    low = (value - high.astype(jnp.float32)).astype(jnp.bfloat16)
    both = jnp.concatenate([high, low], 0)

    def turned(half):
        main = jnp.dot(both, base_hi[half], preferred_element_type=jnp.float32)
        rest = jnp.dot(high, base_lo[half], preferred_element_type=jnp.float32)
        return main[0:24] + (main[32:56] + rest[0:24])

    prod[...] = turned(not_core)
    give_r = pltpu.make_async_remote_copy(
        src_ref=prod, dst_ref=prod_got, send_sem=p_send, recv_sem=p_recv,
        device_id=partner, device_id_type=MESH,
    )
    give_r.start()
    mine = turned(core)
    give_r.wait()
    r_out[...] = mine[0:ROWS] + prod_got[0:ROWS, :]

    for way in range(2):
        for step in range(4):
            for piece in range(PIECES):
                if step > 0 or FIRST[way][piece] is not None:
                    hop(way, step, piece).wait_send()
    for number in range(len(OFFSETS)):
        for piece in range(PIECES):
            over(number, piece).wait_send()


def shards(tokens, factor_old, basis):
    tok_rows, features = tokens.shape
    scale_new = (1.0 - decay_rate) / (tok_rows * lax.axis_size("dp"))
    f32, bf16 = jnp.float32, jnp.bfloat16
    body = lambda *refs: kernel(scale_new, *refs)
    dma = pltpu.SemaphoreType.DMA
    return pl.pallas_call(
        body,
        name="gram_rotate",
        out_shape=(
            jax.ShapeDtypeStruct((ROWS, HALF), f32),
            jax.ShapeDtypeStruct((ROWS, HALF), f32),
        ),
        in_specs=[pl.BlockSpec(memory_space=pl.ANY)] * 3,
        out_specs=[pl.BlockSpec(memory_space=pltpu.VMEM)] * 2,
        scratch_shapes=[
            pltpu.VMEM((tok_rows, HALF), bf16),
            pltpu.VMEM((tok_rows, HALF), bf16),
            pltpu.VMEM((SIDE, PIECES, PAD, WIDE), f32),
            pltpu.VMEM((PIECES, PAD, WIDE), f32),
            pltpu.VMEM((2, 4, PIECES, PAD, WIDE), bf16),
            pltpu.VMEM((2, 4, PIECES, PAD, WIDE), bf16),
            pltpu.VMEM((SIDE, 48 * PIECES, 128), f32),
            pltpu.VMEM((SIDE, 48 * PIECES, 128), bf16),
            pltpu.VMEM((SIDE - 1, 48 * PIECES, 128), bf16),
            pltpu.VMEM((ROWS, HALF), f32),
            pltpu.VMEM((HALF, 2 * HALF), f32),
            pltpu.VMEM((2, HALF, HALF), bf16),
            pltpu.VMEM((2, HALF, HALF), bf16),
            pltpu.VMEM((24, HALF), f32),
            pltpu.VMEM((24, HALF), f32),
            dma((3,)),
            dma((2,)),
            dma((2, 4, PIECES)),
            dma((2, 4, PIECES)),
            dma((SIDE - 1, PIECES)),
            dma((SIDE - 1, PIECES)),
            dma,
            dma,
            pltpu.SemaphoreType.REGULAR((3,)),
        ],
        compiler_params=pltpu.CompilerParams(
            collective_id=0, has_side_effects=True, vmem_limit_bytes=48 * 2**20
        ),
    )(tokens, factor_old, basis)


def solution(mesh):
    return jax.shard_map(
        shards,
        mesh=mesh,
        in_specs=(P("dp", "mp"), P("dp", "mp"), P("mp", None)),
        out_specs=(P("dp", "mp"), P("dp", "mp")),
        check_vma=False,
    )
```

time: 208 us -> 47.1 us (0.23)
  waiting for transfers between devices: 166 us -> 0 us
  Pallas kernels: 0 us -> 40.8 us
  starting transfers between devices: 14.8 us -> 0 us
  between operations: 14.8 us -> 0.65 us
  matrix products: 7.72 us -> 0 us
  local copies, waits for them, and re-layouts: 1.37 us -> 5.37 us
  other arithmetic: 2.66 us -> 0 us
    unnamed x2 -> x0, waiting for transfers between devices: 164 us -> none
    pallas_call x0 -> x1, Pallas kernels: none -> 40.8 us  [shards(): pl.pallas_call(body, name='gram_rotate', out_shape=(jax.ShapeDtypeStruct(...]
    ppermute x2 -> x0, starting transfers between devices: 14.8 us -> none  [partner_2(): return lax.ppermute(block, axis, route)]
    dot_general x2 -> x0, matrix products: 7.72 us -> none  [the longest x1 4.02 us: shards(): partial_sum = jnp.dot(factor_new, basis, precision=lax.Precision.HIGHEST)]
    unnamed x5 -> x7, local copies, waits for them, and re-layouts: 1.28 us -> 5.37 us
    ppermute x2 -> x0, waiting for transfers between devices: 2.34 us -> none  [partner_2(): return lax.ppermute(block, axis, route)]
  transfers between devices with their start and end apart: 3 -> 0, of which waited for: 3 -> 0; matrix products, arithmetic and copies ran while one was open for 1% -> 0% of each run, Pallas kernels for 0% -> 0%
where the time goes in v1:
time: 47.1 us; the launch traced here: 46.9 us
  Pallas kernels  40.8 us (87%)
  local copies, waits for them, and re-layouts  5.37 us (11%)
  between operations  0.65 us (1%)
    pallas_call x1, Pallas kernels, shards(): pl.pallas_call(body, name='gram_rotate', out_shape=(jax.ShapeDtypeStruct(...  40.8 us
    unnamed x7, local copies, waits for them, and re-layouts  5.37 us

profile of v1, /device:TPU:1, one launch (start us, length us, event | category | flops | bytes accessed | tf_op | source)
XLA Modules:
  0.0 46.9 jit_solution(11758225546364945284)
XLA Ops:
  0.6 1.1 %copy.5.refs_0_ = bf16[256,672]{1,0:T(8,128)(2,1)S(1)} copy(bf16[256,672]{0,1:T(8,128)(2,1)} %param.3) | data formatting | bytes 688128 | tf_op args[0]
  1.8 0.0 copy-start
  1.8 2.1 %copy-done = f32[672,1344]{1,0:T(8,128)S(1)} copy-done((f32[672,1344]{1,0:T(8,128)S(1)}, f32[672,1344]{1,0:T(8,128)}, u32[]{:S(2)}) %copy-start) | copy-done | bytes 3612696
  3.9 0.0 copy-start.1
  3.9 0.9 %copy-done.1 = f32[21,672]{1,0:T(8,128)S(1)} copy-done((f32[21,672]{1,0:T(8,128)S(1)}, f32[21,672]{1,0:T(8,128)}, u32[]{:S(2)}) %copy-start.1) | copy-done | bytes 56472
  4.7 40.8 %gram_rotate.1 = (f32[21,672]{1,0:T(8,128)S(1)}, f32[21,672]{1,0:T(8,128)S(1)}) custom-call(bf16[256,672]{1,0:T(8,128)(2,1)S(1)} %copy.5.refs_0_, f32[21,672]{1,0:T(8,128)S(1)} %copy-done.1, f32[672,1344]{1,0:T(8,128)S(1)} %copy-done), custom_call_target="tpu_custom_call" | custom-call | tf_op jit(solution)/shard_map/gram_rotate/pallas_call | solution.py:257
  45.6 0.6 %copy.8 = f32[21,672]{1,0:T(8,128)} copy(f32[21,672]{1,0:T(8,128)S(1)} %get-tuple-element.4) | data formatting | bytes 112896
  46.2 0.6 %copy.9 = f32[21,672]{1,0:T(8,128)} copy(f32[21,672]{1,0:T(8,128)S(1)} %get-tuple-element.5) | data formatting | bytes 112896
Async XLA Ops:
  1.8 2.1 %copy-start = (f32[672,1344]{1,0:T(8,128)S(1)}, f32[672,1344]{1,0:T(8,128)}, u32[]{:S(2)}) copy-start(f32[672,1344]{1,0:T(8,128)} %refs_2_.1) | copy-start | bytes 10838020
  3.9 0.9 %copy-start.1 = (f32[21,672]{1,0:T(8,128)S(1)}, f32[21,672]{1,0:T(8,128)}, u32[]{:S(2)}) copy-start(f32[21,672]{1,0:T(8,128)} %refs_1_.1) | copy-start | bytes 169348

commit v2 on v1

v2 whole, which is shorter than its diff:
```python
import jax
import jax.numpy as jnp
from jax import lax
from jax.experimental import pallas as pl
from jax.experimental.pallas import tpu as pltpu
from jax.sharding import PartitionSpec as P

decay_rate = 0.95

MESH = pl.DeviceIdType.MESH
SIDE = 8
ROWS = 21
CHUNK = SIDE * ROWS
PAD = 176
HALF = 672
FULL = 5
REST = HALF - 128 * FULL
TAIL = FULL * PAD
LONG = TAIL + 48
PIECES = ((0, 352), (352, 704), (704, LONG))
FIRST = ((0, LONG // 2), (LONG // 2, LONG))
RIGHT, LEFT = 0, 1
ORDER = ((2, 0, 1), (0, 2, 1))
LAST = (0, 2, 1)
OFFSETS = (4, 3, -3, 2, -2, 1, -1)


def encode(value):
    return ((value * jnp.abs(value)) * (value * value)).astype(jnp.bfloat16)


def decode(code):
    code = code.astype(jnp.float32)
    root = lax.rsqrt(lax.rsqrt(jnp.abs(code)))
    return jnp.where(code < 0.0, -root, root)


def overlap(one, other):
    lo, hi = max(one[0], other[0]), min(one[1], other[1])
    return (lo, hi) if lo < hi else None


def turn_pieces(both, base_hi, base_lo, half, piece):
    lo, hi = 256 * piece, min(256 * piece + 256, HALF)
    out = jnp.dot(both, base_hi[half, lo:hi, :], preferred_element_type=jnp.float32)
    return out + jnp.dot(both, base_lo[half, lo:hi, :], preferred_element_type=jnp.float32)


def kernel(
    scale_new, tok, old, bas, f_out, r_out,
    own_x, par_x, wide_x, left_x, gram, sums, rest, sent, got, flat, codes, far, fac,
    base, base_hi, base_lo, prod, prod_got,
    load_sem, par_sem, s_send, s_recv, t_send, t_recv, p_send, p_recv, ready,
):
    dp, mp = lax.axis_index("dp"), lax.axis_index("mp")
    y, z, core = dp // SIDE, dp % SIDE, mp % 2
    not_core = 1 - core
    here = not_core * y + core * z
    across = core * y + not_core * z

    def along(step):
        to_y = (y + not_core * step + SIDE) % SIDE
        to_z = (z + core * step + SIDE) % SIDE
        return {"dp": to_y * SIDE + to_z, "mp": mp}

    def cross(step):
        to_y = (y + core * step + SIDE) % SIDE
        to_z = (z + not_core * step + SIDE) % SIDE
        return {"dp": to_y * SIDE + to_z, "mp": mp}

    partner = {"dp": dp, "mp": mp + 1 - 2 * core}

    load_x = pltpu.make_async_copy(tok, own_x, load_sem.at[0])
    load_b = pltpu.make_async_copy(bas, base, load_sem.at[1])
    load_f = pltpu.make_async_copy(old, fac, load_sem.at[2])
    barrier = pltpu.get_barrier_semaphore()
    for device in (partner, along(1), along(-1), cross(1), cross(-1)):
        pl.semaphore_signal(barrier, inc=1, device_id=device, device_id_type=MESH)
    load_x.start()
    wide_x[2 * HALF:2 * HALF + 8, :] = jnp.zeros((8, wide_x.shape[1]), jnp.float32)
    left_x[CHUNK:192, :] = jnp.zeros((192 - CHUNK, wide_x.shape[1]), jnp.float32)
    pl.semaphore_wait(barrier, 5)
    give_x = pltpu.make_async_remote_copy(
        src_ref=tok, dst_ref=par_x, send_sem=par_sem.at[0], recv_sem=par_sem.at[1],
        device_id=partner, device_id_type=MESH,
    )
    give_x.start()
    load_b.start()
    load_f.start()

    def announce(number):
        for device in (cross(1), cross(-1)):
            pl.semaphore_signal(
                ready.at[number], inc=1, device_id=device, device_id_type=MESH
            )

    announce(0)
    load_x.wait()
    wide_x[pl.ds(pl.multiple_of(HALF * core, 8), HALF), :] = own_x[...].astype(jnp.float32)
    give_x.wait()
    wide_x[pl.ds(pl.multiple_of(HALF * not_core, 8), HALF), :] = par_x[...].astype(jnp.float32)

    def products(slot, position):
        for group in range(SIDE):
            in_y = CHUNK * position + ROWS * group
            in_z = ROWS * position + CHUNK * group
            start = not_core * in_y + core * in_z
            block = wide_x[pl.ds(pl.multiple_of(start // 8 * 8, 8), 32), :]
            block = pltpu.roll(block, (32 - start % 8) % 32, 0)
            left_x[ROWS * group:ROWS * group + 24, :] = block[0:24]
        left = left_x[...].astype(jnp.bfloat16)
        main = lax.dot_general(
            left[0:PAD], own_x[0:128 * FULL, :], (((1,), (1,)), ((), ())),
            preferred_element_type=jnp.float32,
        )
        for tile in range(FULL):
            gram[slot, PAD * tile:PAD * (tile + 1), :] = main[:, 128 * tile:128 * (tile + 1)]
        thin = lax.dot_general(
            left, own_x[128 * FULL:HALF, :], (((1,), (1,)), ((), ())),
            preferred_element_type=jnp.float32,
        )
        gram[slot, TAIL:LONG, :] = jnp.concatenate(
            [thin[48 * k:48 * (k + 1)] for k in range(4)], 1
        )

    def slot_of(way, step):
        return 0 if step == 0 else 2 * step - 1 + way

    def rows_of(way, step, piece):
        return overlap(FIRST[way], PIECES[piece]) if step == 0 else PIECES[piece]

    def hop(way, step, piece):
        lo, hi = rows_of(way, step, piece)
        return pltpu.make_async_remote_copy(
            src_ref=sent.at[way, step, pl.ds(lo, hi - lo)],
            dst_ref=got.at[way, step, pl.ds(lo, hi - lo)],
            send_sem=s_send.at[way, step, piece], recv_sem=s_recv.at[way, step, piece],
            device_id=along(1 if way == RIGHT else -1), device_id_type=MESH,
        )

    def put(way, step, piece):
        slot = slot_of(way, step)
        lo, hi = rows_of(way, step, piece)
        arrived = rows_of(way, step - 1, piece) if step else None
        if arrived is None:
            sent[way, step, lo:hi, :] = encode(gram[slot, lo:hi, :])
        else:
            a, b = arrived
            for c, d in ((lo, a), (b, hi)):
                if c < d:
                    sent[way, step, c:d, :] = encode(gram[slot, c:d, :])
            hop(way, step - 1, piece).wait_recv()
            sent[way, step, a:b, :] = encode(
                gram[slot, a:b, :] + decode(got[way, step - 1, a:b, :])
            )
        hop(way, step, piece).start()

    def split_base(first, last):
        @pl.loop(first, last)
        def _(part):
            at = pl.ds(pl.multiple_of(part * 96, 96), 96)
            for half in range(2):
                value = base[at, HALF * half:HALF * (half + 1)]
                high = value.astype(jnp.bfloat16)
                base_hi[half, at, :] = high
                base_lo[half, at, :] = (value - high.astype(jnp.float32)).astype(jnp.bfloat16)

    products(0, (here + 4) % SIDE)
    put(RIGHT, 0, 0)
    put(LEFT, 0, 2)
    put(RIGHT, 0, 1)
    put(LEFT, 0, 1)
    products(1, (here + 3) % SIDE)
    put(RIGHT, 1, ORDER[RIGHT][0])
    products(2, (here + 5) % SIDE)
    put(LEFT, 1, ORDER[LEFT][0])
    products(3, (here + 2) % SIDE)
    products(4, (here + 6) % SIDE)
    for place in (1, 2):
        put(RIGHT, 1, ORDER[RIGHT][place])
        put(LEFT, 1, ORDER[LEFT][place])
    pl.semaphore_wait(ready.at[0], 2)
    announce(1)
    products(5, (here + 1) % SIDE)
    products(6, (here + 7) % SIDE)
    for place in range(3):
        put(RIGHT, 2, ORDER[RIGHT][place])
        put(LEFT, 2, ORDER[LEFT][place])
    pl.semaphore_wait(ready.at[1], 2)
    announce(2)
    products(7, here)
    load_b.wait()
    split_base(0, 4)
    for place in range(3):
        put(RIGHT, 3, ORDER[RIGHT][place])
        put(LEFT, 3, ORDER[LEFT][place])
    split_base(4, 7)
    pl.semaphore_wait(ready.at[2], 2)

    def over(number, piece):
        to = (across + OFFSETS[number] + SIDE) % SIDE
        return pltpu.make_async_remote_copy(
            src_ref=codes.at[to, pl.ds(48 * piece, 48)],
            dst_ref=far.at[number, pl.ds(48 * piece, 48)],
            send_sem=t_send.at[number, piece], recv_sem=t_recv.at[number, piece],
            device_id=cross(OFFSETS[number]), device_id_type=MESH,
        )

    for piece in LAST:
        lo, hi = PIECES[piece]
        hop(RIGHT, 3, piece).wait_recv()
        hop(LEFT, 3, piece).wait_recv()
        sums[lo:hi, :] = (
            gram[7, lo:hi, :] + decode(got[RIGHT, 3, lo:hi, :]) + decode(got[LEFT, 3, lo:hi, :])
        )
        if piece == 2:
            for k in range(4):
                rest[48 * k:48 * (k + 1), 0:REST] = sums[TAIL:LONG, REST * k:REST * (k + 1)]
        for to in range(SIDE):
            parts = []
            for tile in (2 * piece, 2 * piece + 1):
                if tile < FULL:
                    at = PAD * tile + ROWS * to
                    parts.append(sums[at:at + 24, :])
                else:
                    parts.append(rest[ROWS * to:ROWS * to + 24, :])
            both = jnp.concatenate(parts, 0)
            flat[to, 48 * piece:48 * piece + 48, :] = both
            codes[to, 48 * piece:48 * piece + 48, :] = encode(both)
        for number in range(len(OFFSETS)):
            over(number, piece).start()

    load_f.wait()
    fac_rows = []
    theirs = jnp.zeros((48, HALF), jnp.float32)
    mine = jnp.zeros((48, HALF), jnp.float32)
    for piece in LAST:
        total = flat[across, 48 * piece:48 * piece + 48, :]
        for number in range(len(OFFSETS)):
            over(number, piece).wait_recv()
            total += decode(far[number, 48 * piece:48 * piece + 48, :])
        lo, hi = 256 * piece, min(256 * piece + 256, HALF)
        gram_part = jnp.concatenate([total[0:24], total[24:48]], 1)[0:ROWS, 0:hi - lo]
        new = decay_rate * fac[:, lo:hi] + scale_new * gram_part
        f_out[:, lo:hi] = new
        new = jnp.concatenate([new, jnp.zeros((24 - ROWS, hi - lo), jnp.float32)], 0)
        high = new.astype(jnp.bfloat16).astype(jnp.float32)
        both = jnp.concatenate([high, new - high], 0).astype(jnp.bfloat16)
        theirs += turn_pieces(both, base_hi, base_lo, not_core, piece)
        if piece != LAST[-1]:
            mine += turn_pieces(both, base_hi, base_lo, core, piece)

    prod[...] = theirs[0:24] + theirs[24:48]
    give_r = pltpu.make_async_remote_copy(
        src_ref=prod, dst_ref=prod_got, send_sem=p_send, recv_sem=p_recv,
        device_id=partner, device_id_type=MESH,
    )
    give_r.start()
    mine += turn_pieces(both, base_hi, base_lo, core, LAST[-1])
    for way in range(2):
        for step in range(4):
            for piece in range(3):
                if rows_of(way, step, piece) is not None:
                    hop(way, step, piece).wait_send()
    for number in range(len(OFFSETS)):
        for piece in range(3):
            over(number, piece).wait_send()
    give_r.wait()
    r_out[...] = mine[0:ROWS] + mine[24:24 + ROWS] + prod_got[0:ROWS, :]


def shards(tokens, factor_old, basis):
    tok_rows, features = tokens.shape
    scale_new = (1.0 - decay_rate) / (tok_rows * lax.axis_size("dp"))
    f32, bf16 = jnp.float32, jnp.bfloat16
    body = lambda *refs: kernel(scale_new, *refs)
    dma = pltpu.SemaphoreType.DMA
    return pl.pallas_call(
        body,
        name="gram_rotate",
        out_shape=(
            jax.ShapeDtypeStruct((ROWS, HALF), f32),
            jax.ShapeDtypeStruct((ROWS, HALF), f32),
        ),
        in_specs=[pl.BlockSpec(memory_space=pl.ANY)] * 3,
        out_specs=[pl.BlockSpec(memory_space=pltpu.VMEM)] * 2,
        scratch_shapes=[
            pltpu.VMEM((HALF, tok_rows), bf16),
            pltpu.VMEM((HALF, tok_rows), bf16),
            pltpu.VMEM((2 * HALF + 8, tok_rows), f32),
            pltpu.VMEM((192, tok_rows), f32),
            pltpu.VMEM((SIDE, LONG, 128), f32),
            pltpu.VMEM((LONG, 128), f32),
            pltpu.VMEM((192, 128), f32),
            pltpu.VMEM((2, 4, LONG, 128), bf16),
            pltpu.VMEM((2, 4, LONG, 128), bf16),
            pltpu.VMEM((SIDE, 144, 128), f32),
            pltpu.VMEM((SIDE, 144, 128), bf16),
            pltpu.VMEM((SIDE - 1, 144, 128), bf16),
            pltpu.VMEM((ROWS, HALF), f32),
            pltpu.VMEM((HALF, 2 * HALF), f32),
            pltpu.VMEM((2, HALF, HALF), bf16),
            pltpu.VMEM((2, HALF, HALF), bf16),
            pltpu.VMEM((24, HALF), f32),
            pltpu.VMEM((24, HALF), f32),
            dma((3,)),
            dma((2,)),
            dma((2, 4, 3)),
            dma((2, 4, 3)),
            dma((SIDE - 1, 3)),
            dma((SIDE - 1, 3)),
            dma,
            dma,
            pltpu.SemaphoreType.REGULAR((3,)),
        ],
        compiler_params=pltpu.CompilerParams(
            collective_id=0, has_side_effects=True, vmem_limit_bytes=55040 * 1024
        ),
    )(tokens.T, factor_old, basis)


def solution(mesh):
    return jax.shard_map(
        shards,
        mesh=mesh,
        in_specs=(P("dp", "mp"), P("dp", "mp"), P("mp", None)),
        out_specs=(P("dp", "mp"), P("dp", "mp")),
        check_vma=False,
    )
```

time: 47.1 us -> 42.9 us (0.911)
  local copies, waits for them, and re-layouts: 5.37 us -> 1.27 us
    unnamed x7 -> x2, local copies, waits for them, and re-layouts: 5.37 us -> 1.27 us
where the time goes in v2:
time: 42.9 us; the launch traced here: 42.7 us
  Pallas kernels  40.8 us (95%)
  local copies, waits for them, and re-layouts  1.27 us (3%)
  between operations  0.64 us (1%)
    pallas_call x1, Pallas kernels, shards(): pl.pallas_call(body, name='gram_rotate', out_shape=(jax.ShapeDtypeStruct(...  40.8 us
    unnamed x2, local copies, waits for them, and re-layouts  1.27 us

profile of v2, /device:TPU:1, one launch (start us, length us, event | category | flops | bytes accessed | tf_op | source)
XLA Modules:
  0.0 42.7 jit_solution(1783291114853898013)
XLA Ops:
  0.6 40.8 %gram_rotate.1 = (f32[21,672]{1,0:T(8,128)S(1)}, f32[21,672]{1,0:T(8,128)S(1)}) custom-call(bf16[672,256]{1,0:T(8,128)(2,1)} %bitcast.1, f32[21,672]{1,0:T(8,128)} %refs_1_.1, f32[672,1344]{1,0:T(8,128)} %refs_2_.1), custom_call_target="tpu_custom_call" | custom-call | tf_op jit(solution)/shard_map/gram_rotate/pallas_call | solution.py:278
  41.5 0.6 %copy.7 = f32[21,672]{1,0:T(8,128)} copy(f32[21,672]{1,0:T(8,128)S(1)} %get-tuple-element.4) | data formatting | bytes 112896
  42.1 0.6 %copy.8 = f32[21,672]{1,0:T(8,128)} copy(f32[21,672]{1,0:T(8,128)S(1)} %get-tuple-element.5) | data formatting | bytes 112896

commit v3 on v2

--- a/solution.py
+++ b/solution.py
@@ -15,13 +15,15 @@
 HALF = 672
 FULL = 5
 REST = HALF - 128 * FULL
-TAIL = FULL * PAD
-LONG = TAIL + 48
-PIECES = ((0, 352), (352, 704), (704, LONG))
+LONG = FULL * PAD + 48
+TILES = (0, PAD, 2 * PAD, 3 * PAD + 48, 4 * PAD + 48)
+TAIL = 3 * PAD
+PIECES = ((0, PAD), (PAD, 2 * PAD), (2 * PAD, TAIL + 48), (TILES[3], TILES[4]), (TILES[4], LONG))
+GROUPS = ((0, 1), (3, 4), (2,))
+COLUMNS = ((0, 1), (3, 4), (2, 5))
 FIRST = ((0, LONG // 2), (LONG // 2, LONG))
 RIGHT, LEFT = 0, 1
-ORDER = ((2, 0, 1), (0, 2, 1))
-LAST = (0, 2, 1)
+ORDER = ((3, 4, 0, 1, 2), (1, 0, 4, 3, 2))
 OFFSETS = (4, 3, -3, 2, -2, 1, -1)
 
 
@@ -40,10 +42,16 @@
     return (lo, hi) if lo < hi else None
 
 
-def turn_pieces(both, base_hi, base_lo, half, piece):
-    lo, hi = 256 * piece, min(256 * piece + 256, HALF)
-    out = jnp.dot(both, base_hi[half, lo:hi, :], preferred_element_type=jnp.float32)
-    return out + jnp.dot(both, base_lo[half, lo:hi, :], preferred_element_type=jnp.float32)
+def spans(group):
+    return [(128 * tile, min(128 * tile + 128, HALF)) for tile in COLUMNS[group]]
+
+
+def turned(both, base_hi, base_lo, half, group):
+    out = jnp.zeros((48, HALF), jnp.float32)
+    for part, (lo, hi) in zip(both, spans(group)):
+        out += jnp.dot(part, base_hi[half, lo:hi, :], preferred_element_type=jnp.float32)
+        out += jnp.dot(part, base_lo[half, lo:hi, :], preferred_element_type=jnp.float32)
+    return out
 
 
 def kernel(
@@ -114,12 +122,12 @@
             preferred_element_type=jnp.float32,
         )
         for tile in range(FULL):
-            gram[slot, PAD * tile:PAD * (tile + 1), :] = main[:, 128 * tile:128 * (tile + 1)]
+            gram[slot, TILES[tile]:TILES[tile] + PAD, :] = main[:, 128 * tile:128 * (tile + 1)]
         thin = lax.dot_general(
             left, own_x[128 * FULL:HALF, :], (((1,), (1,)), ((), ())),
             preferred_element_type=jnp.float32,
         )
-        gram[slot, TAIL:LONG, :] = jnp.concatenate(
+        gram[slot, TAIL:TAIL + 48, :] = jnp.concatenate(
             [thin[48 * k:48 * (k + 1)] for k in range(4)], 1
         )
 
@@ -165,90 +173,98 @@
                 base_hi[half, at, :] = high
                 base_lo[half, at, :] = (value - high.astype(jnp.float32)).astype(jnp.bfloat16)
 
+    def both_ways(step, places):
+        for place in places:
+            put(RIGHT, step, ORDER[RIGHT][place])
+            put(LEFT, step, ORDER[LEFT][place])
+
     products(0, (here + 4) % SIDE)
-    put(RIGHT, 0, 0)
-    put(LEFT, 0, 2)
-    put(RIGHT, 0, 1)
-    put(LEFT, 0, 1)
+    for place in range(3):
+        put(RIGHT, 0, (0, 1, 2)[place])
+        put(LEFT, 0, (4, 3, 2)[place])
     products(1, (here + 3) % SIDE)
-    put(RIGHT, 1, ORDER[RIGHT][0])
     products(2, (here + 5) % SIDE)
-    put(LEFT, 1, ORDER[LEFT][0])
+    both_ways(1, (0, 1))
     products(3, (here + 2) % SIDE)
     products(4, (here + 6) % SIDE)
-    for place in (1, 2):
-        put(RIGHT, 1, ORDER[RIGHT][place])
-        put(LEFT, 1, ORDER[LEFT][place])
+    both_ways(1, (2, 3, 4))
     pl.semaphore_wait(ready.at[0], 2)
     announce(1)
     products(5, (here + 1) % SIDE)
     products(6, (here + 7) % SIDE)
-    for place in range(3):
-        put(RIGHT, 2, ORDER[RIGHT][place])
-        put(LEFT, 2, ORDER[LEFT][place])
+    both_ways(2, range(5))
     pl.semaphore_wait(ready.at[1], 2)
     announce(2)
     products(7, here)
     load_b.wait()
     split_base(0, 4)
-    for place in range(3):
-        put(RIGHT, 3, ORDER[RIGHT][place])
-        put(LEFT, 3, ORDER[LEFT][place])
+    both_ways(3, range(5))
     split_base(4, 7)
     pl.semaphore_wait(ready.at[2], 2)
 
-    def over(number, piece):
-        to = (across + OFFSETS[number] + SIDE) % SIDE
+    def over(number, group):
+        to = core * ((across + OFFSETS[number] + SIDE) % SIDE) + not_core * (
+            number + jnp.where(across <= number, 1, 0)
+        )
+        away = (to - across + SIDE) % SIDE
+        at = pl.ds(48 * group, 48)
         return pltpu.make_async_remote_copy(
-            src_ref=codes.at[to, pl.ds(48 * piece, 48)],
-            dst_ref=far.at[number, pl.ds(48 * piece, 48)],
-            send_sem=t_send.at[number, piece], recv_sem=t_recv.at[number, piece],
-            device_id=cross(OFFSETS[number]), device_id_type=MESH,
-        )
-
-    for piece in LAST:
-        lo, hi = PIECES[piece]
-        hop(RIGHT, 3, piece).wait_recv()
-        hop(LEFT, 3, piece).wait_recv()
-        sums[lo:hi, :] = (
-            gram[7, lo:hi, :] + decode(got[RIGHT, 3, lo:hi, :]) + decode(got[LEFT, 3, lo:hi, :])
-        )
-        if piece == 2:
+            src_ref=codes.at[to, at], dst_ref=far.at[away - 1, at],
+            send_sem=t_send.at[away - 1, group], recv_sem=t_recv.at[away - 1, group],
+            device_id=cross(away), device_id_type=MESH,
+        )
+
+    def landed(slot, group):
+        at = pl.ds(48 * group, 48)
+        return pltpu.make_async_remote_copy(
+            src_ref=codes.at[0, at], dst_ref=far.at[slot, at],
+            send_sem=t_send.at[slot, group], recv_sem=t_recv.at[slot, group],
+            device_id=cross(slot + 1), device_id_type=MESH,
+        )
+
+    for group, pieces in enumerate(GROUPS):
+        for piece in pieces:
+            lo, hi = PIECES[piece]
+            hop(RIGHT, 3, piece).wait_recv()
+            hop(LEFT, 3, piece).wait_recv()
+            sums[lo:hi, :] = (
+                gram[7, lo:hi, :] + decode(got[RIGHT, 3, lo:hi, :]) + decode(got[LEFT, 3, lo:hi, :])
+            )
+        if 2 in pieces:
             for k in range(4):
-                rest[48 * k:48 * (k + 1), 0:REST] = sums[TAIL:LONG, REST * k:REST * (k + 1)]
+                rest[48 * k:48 * (k + 1), 0:REST] = sums[TAIL:TAIL + 48, REST * k:REST * (k + 1)]
         for to in range(SIDE):
             parts = []
-            for tile in (2 * piece, 2 * piece + 1):
+            for tile in COLUMNS[group]:
                 if tile < FULL:
-                    at = PAD * tile + ROWS * to
+                    at = TILES[tile] + ROWS * to
                     parts.append(sums[at:at + 24, :])
                 else:
                     parts.append(rest[ROWS * to:ROWS * to + 24, :])
             both = jnp.concatenate(parts, 0)
-            flat[to, 48 * piece:48 * piece + 48, :] = both
-            codes[to, 48 * piece:48 * piece + 48, :] = encode(both)
-        for number in range(len(OFFSETS)):
-            over(number, piece).start()
+            flat[to, 48 * group:48 * group + 48, :] = both
+            codes[to, 48 * group:48 * group + 48, :] = encode(both)
+        for number in range(SIDE - 1):
+            over(number, group).start()
 
     load_f.wait()
-    fac_rows = []
     theirs = jnp.zeros((48, HALF), jnp.float32)
     mine = jnp.zeros((48, HALF), jnp.float32)
-    for piece in LAST:
-        total = flat[across, 48 * piece:48 * piece + 48, :]
-        for number in range(len(OFFSETS)):
-            over(number, piece).wait_recv()
-            total += decode(far[number, 48 * piece:48 * piece + 48, :])
-        lo, hi = 256 * piece, min(256 * piece + 256, HALF)
-        gram_part = jnp.concatenate([total[0:24], total[24:48]], 1)[0:ROWS, 0:hi - lo]
-        new = decay_rate * fac[:, lo:hi] + scale_new * gram_part
-        f_out[:, lo:hi] = new
-        new = jnp.concatenate([new, jnp.zeros((24 - ROWS, hi - lo), jnp.float32)], 0)
-        high = new.astype(jnp.bfloat16).astype(jnp.float32)
-        both = jnp.concatenate([high, new - high], 0).astype(jnp.bfloat16)
-        theirs += turn_pieces(both, base_hi, base_lo, not_core, piece)
-        if piece != LAST[-1]:
-            mine += turn_pieces(both, base_hi, base_lo, core, piece)
+    for group in range(3):
+        total = flat[across, 48 * group:48 * group + 48, :]
+        for slot in range(SIDE - 1):
+            landed(slot, group).wait_recv()
+            total += decode(far[slot, 48 * group:48 * group + 48, :])
+        both = []
+        for k, (lo, hi) in enumerate(spans(group)):
+            new = decay_rate * fac[:, lo:hi] + scale_new * total[24 * k:24 * k + ROWS, 0:hi - lo]
+            f_out[:, lo:hi] = new
+            new = jnp.concatenate([new, jnp.zeros((24 - ROWS, hi - lo), jnp.float32)], 0)
+            high = new.astype(jnp.bfloat16).astype(jnp.float32)
+            both.append(jnp.concatenate([high, new - high], 0).astype(jnp.bfloat16))
+        theirs += turned(both, base_hi, base_lo, not_core, group)
+        if group < 2:
+            mine += turned(both, base_hi, base_lo, core, group)
 
     prod[...] = theirs[0:24] + theirs[24:48]
     give_r = pltpu.make_async_remote_copy(
@@ -256,15 +272,15 @@
         device_id=partner, device_id_type=MESH,
     )
     give_r.start()
-    mine += turn_pieces(both, base_hi, base_lo, core, LAST[-1])
+    mine += turned(both, base_hi, base_lo, core, 2)
     for way in range(2):
         for step in range(4):
-            for piece in range(3):
+            for piece in range(5):
                 if rows_of(way, step, piece) is not None:
                     hop(way, step, piece).wait_send()
-    for number in range(len(OFFSETS)):
-        for piece in range(3):
-            over(number, piece).wait_send()
+    for number in range(SIDE - 1):
+        for group in range(3):
+            over(number, group).wait_send()
     give_r.wait()
     r_out[...] = mine[0:ROWS] + mine[24:24 + ROWS] + prod_got[0:ROWS, :]
 
@@ -305,8 +321,8 @@
             pltpu.VMEM((24, HALF), f32),
             dma((3,)),
             dma((2,)),
-            dma((2, 4, 3)),
-            dma((2, 4, 3)),
+            dma((2, 4, 5)),
+            dma((2, 4, 5)),
             dma((SIDE - 1, 3)),
             dma((SIDE - 1, 3)),
             dma,

time: 42.9 us -> 40.7 us (0.949)
  Pallas kernels: 40.8 us -> 38.7 us
    pallas_call x1, Pallas kernels: 40.8 us -> 38.7 us  [shards(): pl.pallas_call(body, name='gram_rotate', out_shape=(jax.ShapeDtypeStruct(...]
where the time goes in v3:
time: 40.7 us; the launch traced here: 40.6 us
  Pallas kernels  38.7 us (95%)
  local copies, waits for them, and re-layouts  1.27 us (3%)
  between operations  0.64 us (2%)
    pallas_call x1, Pallas kernels, shards(): pl.pallas_call(body, name='gram_rotate', out_shape=(jax.ShapeDtypeStruct(...  38.7 us
    unnamed x2, local copies, waits for them, and re-layouts  1.27 us

profile of v3, /device:TPU:1, one launch (start us, length us, event | category | flops | bytes accessed | tf_op | source)
XLA Modules:
  0.0 40.6 jit_solution(1717247979339606415)
XLA Ops:
  0.6 38.7 %gram_rotate.1 = (f32[21,672]{1,0:T(8,128)S(1)}, f32[21,672]{1,0:T(8,128)S(1)}) custom-call(bf16[672,256]{1,0:T(8,128)(2,1)} %bitcast.1, f32[21,672]{1,0:T(8,128)} %refs_1_.1, f32[672,1344]{1,0:T(8,128)} %refs_2_.1), custom_call_target="tpu_custom_call" | custom-call | tf_op jit(solution)/shard_map/gram_rotate/pallas_call | solution.py:294
  39.3 0.6 %copy.7 = f32[21,672]{1,0:T(8,128)} copy(f32[21,672]{1,0:T(8,128)S(1)} %get-tuple-element.4) | data formatting | bytes 112896
  40.0 0.6 %copy.8 = f32[21,672]{1,0:T(8,128)} copy(f32[21,672]{1,0:T(8,128)S(1)} %get-tuple-element.5) | data formatting | bytes 112896

commit v4 on v3

v4 whole, which is shorter than its diff:
```python
import jax
import jax.numpy as jnp
from jax import lax
from jax.experimental import pallas as pl
from jax.experimental.pallas import tpu as pltpu
from jax.sharding import PartitionSpec as P

decay_rate = 0.95

MESH = pl.DeviceIdType.MESH
SIDE = 8
ROWS = 21
CHUNK = SIDE * ROWS
HALF = 672
FULL = 5
REST = HALF - 128 * FULL
TILES = (0, CHUNK, 2 * CHUNK, 3 * CHUNK + 56, 4 * CHUNK + 56)
TAIL = 3 * CHUNK
LONG = 5 * CHUNK + 56
PIECES = ((0, 176), (176, 336), (336, 560), (560, 720), (720, LONG))
SUBS = ((0, 176), (176, 336), (336, 448), (448, 560), (560, 720), (720, LONG))
SUBS_OF = ((0,), (1,), (2, 3), (4,), (5,))
GROUPS = ((0, 1), (3, 4), (2,))
COLUMNS = ((0, 1), (3, 4), (2, 5))
RIGHT, LEFT = 0, 1
FAR = (4, 3, 5)
NEAR = (2, 6, 1, 7)
FIRST = (0, 1)


def encode(value):
    return ((value * jnp.abs(value)) * (value * value)).astype(jnp.bfloat16)


def decode(code):
    code = code.astype(jnp.float32)
    root = lax.rsqrt(lax.rsqrt(jnp.abs(code)))
    return jnp.where(code < 0.0, -root, root)


def spans(group):
    return [(128 * tile, min(128 * tile + 128, HALF)) for tile in COLUMNS[group]]


def turned(both, base_hi, base_lo, half, group):
    out = jnp.zeros((48, HALF), jnp.float32)
    for part, (lo, hi) in zip(both, spans(group)):
        out += jnp.dot(part, base_hi[half, lo:hi, :], preferred_element_type=jnp.float32)
        out += jnp.dot(part, base_lo[half, lo:hi, :], preferred_element_type=jnp.float32)
    return out


def kernel(
    scale_new, tok, old, bas, f_out, r_out,
    own_x, par_x, wide_x, left_x, gram, sums, rest, sent0, got0, sent, got, flat, codes, far, fac,
    base, base_hi, base_lo, prod, prod_got,
    load_sem, par_sem, z_send, z_recv, s_send, s_recv, t_send, t_recv, w_send, w_recv,
    p_send, p_recv, ready, hello, go,
):
    dp, mp = lax.axis_index("dp"), lax.axis_index("mp")
    y, z, core = dp // SIDE, dp % SIDE, mp % 2
    not_core = 1 - core
    here = not_core * y + core * z
    across = core * y + not_core * z

    def along(step):
        to_y = (y + not_core * step + SIDE) % SIDE
        to_z = (z + core * step + SIDE) % SIDE
        return {"dp": to_y * SIDE + to_z, "mp": mp}

    def cross(step):
        to_y = (y + core * step + SIDE) % SIDE
        to_z = (z + not_core * step + SIDE) % SIDE
        return {"dp": to_y * SIDE + to_z, "mp": mp}

    partner = {"dp": dp, "mp": mp + 1 - 2 * core}

    load_x = pltpu.make_async_copy(tok, own_x, load_sem.at[0])
    load_b = pltpu.make_async_copy(bas, base, load_sem.at[1])
    load_f = pltpu.make_async_copy(old, fac, load_sem.at[2])
    load_x.start()
    barrier = pltpu.get_barrier_semaphore()
    for step in (1, -1):
        for to_y, to_z in (((y + step + SIDE) % SIDE, z), (y, (z + step + SIDE) % SIDE)):
            pl.semaphore_signal(
                barrier, inc=1, device_id={"dp": to_y * SIDE + to_z, "mp": mp - core},
                device_id_type=MESH,
            )
    give_x = pltpu.make_async_remote_copy(
        src_ref=tok, dst_ref=par_x, send_sem=par_sem.at[0], recv_sem=par_sem.at[1],
        device_id=partner, device_id_type=MESH,
    )

    @pl.when(core == 1)
    def _():
        pl.semaphore_wait(barrier, 1)
        pl.semaphore_signal(hello, inc=1, device_id=partner, device_id_type=MESH)
        give_x.start()

    @pl.when(core == 0)
    def _():
        pl.semaphore_signal(barrier, inc=1, device_id=partner, device_id_type=MESH)
        pl.semaphore_wait(hello, 1)
        give_x.start()

    load_b.start()
    load_f.start()
    wide_x[2 * HALF:2 * HALF + 8, :] = jnp.zeros((8, wide_x.shape[1]), jnp.float32)
    left_x[CHUNK:192, :] = jnp.zeros((192 - CHUNK, wide_x.shape[1]), jnp.float32)
    sums[LONG:LONG + 8, :] = jnp.zeros((8, 128), jnp.float32)
    for slot in range(SIDE):
        gram[slot, TAIL + 48:TAIL + 56, :] = jnp.zeros((8, 128), jnp.float32)

    def announce(number):
        for device in (cross(1), cross(-1)):
            pl.semaphore_signal(
                ready.at[number], inc=1, device_id=device, device_id_type=MESH
            )

    load_x.wait()
    wide_x[pl.ds(pl.multiple_of(HALF * core, 8), HALF), :] = own_x[...].astype(jnp.float32)
    give_x.wait_recv()
    wide_x[pl.ds(pl.multiple_of(HALF * not_core, 8), HALF), :] = par_x[...].astype(jnp.float32)

    def products(slot, position):
        for group in range(SIDE):
            in_y = CHUNK * position + ROWS * group
            in_z = ROWS * position + CHUNK * group
            start = not_core * in_y + core * in_z
            block = wide_x[pl.ds(pl.multiple_of(start // 8 * 8, 8), 32), :]
            block = pltpu.roll(block, (32 - start % 8) % 32, 0)
            left_x[ROWS * group:ROWS * group + 24, :] = block[0:24]
        left = left_x[...].astype(jnp.bfloat16)
        main = lax.dot_general(
            left[0:176], own_x[0:128 * FULL, :], (((1,), (1,)), ((), ())),
            preferred_element_type=jnp.float32,
        )
        for tile in range(FULL):
            gram[slot, TILES[tile]:TILES[tile] + CHUNK, :] = main[0:CHUNK, 128 * tile:128 * (tile + 1)]
        thin = lax.dot_general(
            left, own_x[128 * FULL:HALF, :], (((1,), (1,)), ((), ())),
            preferred_element_type=jnp.float32,
        )
        gram[slot, TAIL:TAIL + 48, :] = jnp.concatenate(
            [thin[48 * k:48 * (k + 1)] for k in range(4)], 1
        )

    def slot_of(way, step):
        return 0 if step == 0 else 2 * step - 1 + way

    def hop0(way, sub):
        lo, hi = SUBS[sub]
        return pltpu.make_async_remote_copy(
            src_ref=sent0.at[pl.ds(lo, hi - lo)], dst_ref=got0.at[pl.ds(lo, hi - lo)],
            send_sem=z_send.at[sub], recv_sem=z_recv.at[sub],
            device_id=along(1 if way == RIGHT else -1), device_id_type=MESH,
        )

    def hop(way, step, piece):
        lo, hi = PIECES[piece]
        return pltpu.make_async_remote_copy(
            src_ref=sent.at[way, step - 1, pl.ds(lo, hi - lo)],
            dst_ref=got.at[way, step - 1, pl.ds(lo, hi - lo)],
            send_sem=s_send.at[way, step - 1, piece], recv_sem=s_recv.at[way, step - 1, piece],
            device_id=along(1 if way == RIGHT else -1), device_id_type=MESH,
        )

    def put(way, step, piece, first=()):
        slot = slot_of(way, step)
        lo, hi = PIECES[piece]
        if step == 1:
            for sub in SUBS_OF[piece]:
                a, b = SUBS[sub]
                total = gram[slot, a:b, :]
                if sub in first:
                    hop0(way, sub).wait_recv()
                    total = total + decode(got0[a:b, :])
                sent[way, 0, a:b, :] = encode(total)
        else:
            hop(way, step - 1, piece).wait_recv()
            sent[way, step - 1, lo:hi, :] = encode(
                gram[slot, lo:hi, :] + decode(got[way, step - 2, lo:hi, :])
            )
        hop(way, step, piece).start()

    def split_base(first, last):
        @pl.loop(first, last)
        def _(part):
            at = pl.ds(pl.multiple_of(part * 96, 96), 96)
            for half in range(2):
                value = base[at, HALF * half:HALF * (half + 1)]
                high = value.astype(jnp.bfloat16)
                base_hi[half, at, :] = high
                base_lo[half, at, :] = (value - high.astype(jnp.float32)).astype(jnp.bfloat16)

    every = (0, 1, 3, 4, 2)
    ahead = ((3, 4, 0, 1, 2), (1, 0, 4, 3, 2))

    products(0, (here + 4) % SIDE)
    sent0[...] = encode(gram[0])

    @pl.when(core == 0)
    def _():
        pl.semaphore_wait(barrier, 8)
        pl.semaphore_signal(go, inc=1, device_id=partner, device_id_type=MESH)
        for right, left in ((0, 5), (1, 4), (2, 3)):
            hop0(RIGHT, right).start()
            hop0(LEFT, left).start()

    @pl.when(core == 1)
    def _():
        pl.semaphore_wait(go, 1)
        for sub in (0, 1, 4, 5, 2, 3):
            hop0(LEFT, sub).start()

    announce(0)
    products(1, (here + 3) % SIDE)
    products(2, (here + 5) % SIDE)

    @pl.when(core == 0)
    def _():
        for place in (0, 1):
            put(RIGHT, 1, ahead[RIGHT][place])
            put(LEFT, 1, ahead[LEFT][place])

    @pl.when(core == 1)
    def _():
        for piece in every:
            put(RIGHT, 1, piece)

    products(3, (here + 2) % SIDE)
    products(4, (here + 6) % SIDE)

    @pl.when(core == 0)
    def _():
        for place in (2, 3, 4):
            put(RIGHT, 1, ahead[RIGHT][place], (0, 1, 2))
            put(LEFT, 1, ahead[LEFT][place], (3, 4, 5))

    @pl.when(core == 1)
    def _():
        for piece in every:
            put(RIGHT, 2, piece)
            put(LEFT, 1, piece, range(6))

    pl.semaphore_wait(ready.at[0], 2)
    announce(1)
    products(5, (here + 1) % SIDE)
    products(6, (here + 7) % SIDE)

    @pl.when(core == 0)
    def _():
        for place in range(5):
            put(RIGHT, 2, ahead[RIGHT][place])
            put(LEFT, 2, ahead[LEFT][place])

    @pl.when(core == 1)
    def _():
        for piece in every:
            put(RIGHT, 3, piece)
            put(LEFT, 2, piece)

    pl.semaphore_wait(ready.at[1], 2)
    announce(2)
    products(7, here)
    load_b.wait()
    split_base(0, 4)

    @pl.when(core == 0)
    def _():
        for place in range(5):
            put(RIGHT, 3, ahead[RIGHT][place])
            put(LEFT, 3, ahead[LEFT][place])

    @pl.when(core == 1)
    def _():
        for piece in every:
            put(LEFT, 3, piece)

    split_base(4, 7)
    pl.semaphore_wait(ready.at[2], 2)

    def over(to, group):
        away = (to - across + SIDE) % SIDE
        slot = away - 1
        if group is None:
            at, send, recv = pl.ds(0, 144), w_send.at[slot], w_recv.at[slot]
        else:
            at, send, recv = pl.ds(48 * group, 48), t_send.at[slot, group], t_recv.at[slot, group]
        return pltpu.make_async_remote_copy(
            src_ref=codes.at[to, at], dst_ref=far.at[slot, at], send_sem=send, recv_sem=recv,
            device_id=cross(away), device_id_type=MESH,
        )

    def each_over(group, act):
        @pl.when(core == 0)
        def _():
            for to in range(SIDE):
                if (to in FIRST) == (group is not None):
                    @pl.when(across != to)
                    def _():
                        act(over(to, group))

        @pl.when(core == 1)
        def _():
            for step in NEAR if group is None else FAR:
                act(over((across + step) % SIDE, group))

    def landed(group):
        def one(step):
            over((across + step) % SIDE, group).wait_recv()

        def whole(step):
            if group == 0:
                over((across + step) % SIDE, None).wait_recv()

        @pl.when(core == 1)
        def _():
            for step in FAR:
                one(step)
            for step in NEAR:
                whole(step)

        @pl.when((core == 0) & (across < len(FIRST)))
        def _():
            for step in range(1, SIDE):
                one(step)

        @pl.when((core == 0) & (across >= len(FIRST)))
        def _():
            for step in range(1, SIDE):
                whole(step)

    for group, pieces in enumerate(GROUPS):
        for piece in pieces:
            lo, hi = PIECES[piece]
            hop(RIGHT, 3, piece).wait_recv()
            hop(LEFT, 3, piece).wait_recv()
            sums[lo:hi, :] = (
                gram[7, lo:hi, :] + decode(got[RIGHT, 2, lo:hi, :]) + decode(got[LEFT, 2, lo:hi, :])
            )
        if 2 in pieces:
            for k in range(4):
                rest[48 * k:48 * (k + 1), 0:REST] = sums[TAIL:TAIL + 48, REST * k:REST * (k + 1)]
        for to in range(SIDE):
            parts = []
            for tile in COLUMNS[group]:
                if tile < FULL:
                    at = TILES[tile] + ROWS * to
                    parts.append(sums[at:at + 24, :])
                else:
                    parts.append(rest[ROWS * to:ROWS * to + 24, :])
            both = jnp.concatenate(parts, 0)
            flat[to, 48 * group:48 * group + 48, :] = both
            codes[to, 48 * group:48 * group + 48, :] = encode(both)
        each_over(group, lambda copy: copy.start())
    each_over(None, lambda copy: copy.start())

    load_f.wait()
    theirs = jnp.zeros((48, HALF), jnp.float32)
    mine = jnp.zeros((48, HALF), jnp.float32)
    for group in range(3):
        total = flat[across, 48 * group:48 * group + 48, :]
        landed(group)
        for slot in range(SIDE - 1):
            total += decode(far[slot, 48 * group:48 * group + 48, :])
        both = []
        for k, (lo, hi) in enumerate(spans(group)):
            new = decay_rate * fac[:, lo:hi] + scale_new * total[24 * k:24 * k + ROWS, 0:hi - lo]
            f_out[:, lo:hi] = new
            new = jnp.concatenate([new, jnp.zeros((24 - ROWS, hi - lo), jnp.float32)], 0)
            high = new.astype(jnp.bfloat16).astype(jnp.float32)
            both.append(jnp.concatenate([high, new - high], 0).astype(jnp.bfloat16))
        theirs += turned(both, base_hi, base_lo, not_core, group)
        if group < 2:
            mine += turned(both, base_hi, base_lo, core, group)

    prod[...] = theirs[0:24] + theirs[24:48]
    give_r = pltpu.make_async_remote_copy(
        src_ref=prod, dst_ref=prod_got, send_sem=p_send, recv_sem=p_recv,
        device_id=partner, device_id_type=MESH,
    )
    give_r.start()
    mine += turned(both, base_hi, base_lo, core, 2)
    give_x.wait_send()

    @pl.when(core == 0)
    def _():
        for sub in range(6):
            hop0(RIGHT if sub < 3 else LEFT, sub).wait_send()

    @pl.when(core == 1)
    def _():
        for sub in range(6):
            hop0(LEFT, sub).wait_send()

    for way in range(2):
        for step in (1, 2, 3):
            for piece in range(5):
                hop(way, step, piece).wait_send()
    for group in (0, 1, 2, None):
        each_over(group, lambda copy: copy.wait_send())
    give_r.wait()
    r_out[...] = mine[0:ROWS] + mine[24:24 + ROWS] + prod_got[0:ROWS, :]


def shards(tokens, factor_old, basis):
    tok_rows, features = tokens.shape
    scale_new = (1.0 - decay_rate) / (tok_rows * lax.axis_size("dp"))
    f32, bf16 = jnp.float32, jnp.bfloat16
    body = lambda *refs: kernel(scale_new, *refs)
    dma = pltpu.SemaphoreType.DMA
    return pl.pallas_call(
        body,
        name="gram_rotate",
        out_shape=(
            jax.ShapeDtypeStruct((ROWS, HALF), f32),
            jax.ShapeDtypeStruct((ROWS, HALF), f32),
        ),
        in_specs=[pl.BlockSpec(memory_space=pl.ANY)] * 3,
        out_specs=[pl.BlockSpec(memory_space=pltpu.VMEM)] * 2,
        scratch_shapes=[
            pltpu.VMEM((HALF, tok_rows), bf16),
            pltpu.VMEM((HALF, tok_rows), bf16),
            pltpu.VMEM((2 * HALF + 8, tok_rows), f32),
            pltpu.VMEM((192, tok_rows), f32),
            pltpu.VMEM((SIDE, LONG, 128), f32),
            pltpu.VMEM((LONG + 8, 128), f32),
            pltpu.VMEM((192, 128), f32),
            pltpu.VMEM((LONG, 128), bf16),
            pltpu.VMEM((LONG, 128), bf16),
            pltpu.VMEM((2, 3, LONG, 128), bf16),
            pltpu.VMEM((2, 3, LONG, 128), bf16),
            pltpu.VMEM((SIDE, 144, 128), f32),
            pltpu.VMEM((SIDE, 144, 128), bf16),
            pltpu.VMEM((SIDE - 1, 144, 128), bf16),
            pltpu.VMEM((ROWS, HALF), f32),
            pltpu.VMEM((HALF, 2 * HALF), f32),
            pltpu.VMEM((2, HALF, HALF), bf16),
            pltpu.VMEM((2, HALF, HALF), bf16),
            pltpu.VMEM((24, HALF), f32),
            pltpu.VMEM((24, HALF), f32),
            dma((3,)),
            dma((2,)),
            dma((6,)),
            dma((6,)),
            dma((2, 3, 5)),
            dma((2, 3, 5)),
            dma((SIDE - 1, 3)),
            dma((SIDE - 1, 3)),
            dma((SIDE - 1,)),
            dma((SIDE - 1,)),
            dma,
            dma,
            pltpu.SemaphoreType.REGULAR((3,)),
            pltpu.SemaphoreType.REGULAR,
            pltpu.SemaphoreType.REGULAR,
        ],
        compiler_params=pltpu.CompilerParams(
            collective_id=0, has_side_effects=True, vmem_limit_bytes=55040 * 1024
        ),
    )(tokens.T, factor_old, basis)


def solution(mesh):
    return jax.shard_map(
        shards,
        mesh=mesh,
        in_specs=(P("dp", "mp"), P("dp", "mp"), P("mp", None)),
        out_specs=(P("dp", "mp"), P("dp", "mp")),
        check_vma=False,
    )
```

time: 40.7 us -> 39.7 us (0.975)
  Pallas kernels: 38.7 us -> 37.7 us
    pallas_call x1, Pallas kernels: 38.7 us -> 37.7 us  [shards(): pl.pallas_call(body, name='gram_rotate', out_shape=(jax.ShapeDtypeStruct(...]
where the time goes in v4:
time: 39.7 us; the launch traced here: 39.6 us
  Pallas kernels  37.7 us (95%)
  local copies, waits for them, and re-layouts  1.27 us (3%)
  between operations  0.64 us (2%)
    pallas_call x1, Pallas kernels, shards(): pl.pallas_call(body, name='gram_rotate', out_shape=(jax.ShapeDtypeStruct(...  37.7 us
    unnamed x2, local copies, waits for them, and re-layouts  1.27 us

profile of v4, /device:TPU:1, one launch (start us, length us, event | category | flops | bytes accessed | tf_op | source)
XLA Modules:
  0.0 39.6 jit_solution(15172784797278532819)
XLA Ops:
  0.6 37.7 %gram_rotate.1 = (f32[21,672]{1,0:T(8,128)S(1)}, f32[21,672]{1,0:T(8,128)S(1)}) custom-call(bf16[672,256]{1,0:T(8,128)(2,1)} %bitcast.1, f32[21,672]{1,0:T(8,128)} %refs_1_.1, f32[672,1344]{1,0:T(8,128)} %refs_2_.1), custom_call_target="tpu_custom_call" | custom-call | tf_op jit(solution)/shard_map/gram_rotate/pallas_call | solution.py:413
  38.3 0.6 %copy.7 = f32[21,672]{1,0:T(8,128)} copy(f32[21,672]{1,0:T(8,128)S(1)} %get-tuple-element.4) | data formatting | bytes 112896
  39.0 0.6 %copy.8 = f32[21,672]{1,0:T(8,128)} copy(f32[21,672]{1,0:T(8,128)S(1)} %get-tuple-element.5) | data formatting | bytes 112896

commit v5 on v4

--- a/solution.py
+++ b/solution.py
@@ -54,7 +54,7 @@
     scale_new, tok, old, bas, f_out, r_out,
     own_x, par_x, wide_x, left_x, gram, sums, rest, sent0, got0, sent, got, flat, codes, far, fac,
     base, base_hi, base_lo, prod, prod_got,
-    load_sem, par_sem, z_send, z_recv, s_send, s_recv, t_send, t_recv, w_send, w_recv,
+    load_sem, par_sem, z_send, z_recv, s_send, s_recv, t_send, t_recv,
     p_send, p_recv, ready, hello, go,
 ):
     dp, mp = lax.axis_index("dp"), lax.axis_index("mp")
@@ -119,8 +119,13 @@
 
     load_x.wait()
     wide_x[pl.ds(pl.multiple_of(HALF * core, 8), HALF), :] = own_x[...].astype(jnp.float32)
-    give_x.wait_recv()
-    wide_x[pl.ds(pl.multiple_of(HALF * not_core, 8), HALF), :] = par_x[...].astype(jnp.float32)
+    alone = (core == 0) & (y >= SIDE // 2)
+
+    def take_x():
+        give_x.wait_recv()
+        wide_x[pl.ds(pl.multiple_of(HALF * not_core, 8), HALF), :] = par_x[...].astype(jnp.float32)
+
+    pl.when(jnp.logical_not(alone))(take_x)
 
     def products(slot, position):
         for group in range(SIDE):
@@ -196,11 +201,13 @@
     every = (0, 1, 3, 4, 2)
     ahead = ((3, 4, 0, 1, 2), (1, 0, 4, 3, 2))
 
-    products(0, (here + 4) % SIDE)
-    sent0[...] = encode(gram[0])
-
-    @pl.when(core == 0)
-    def _():
+    def first_chunk():
+        products(0, (here + 4) % SIDE)
+        sent0[...] = encode(gram[0])
+
+    @pl.when(core == 0)
+    def _():
+        first_chunk()
         pl.semaphore_wait(barrier, 8)
         pl.semaphore_signal(go, inc=1, device_id=partner, device_id_type=MESH)
         for right, left in ((0, 5), (1, 4), (2, 3)):
@@ -209,12 +216,21 @@
 
     @pl.when(core == 1)
     def _():
+        products(1, (here + 3) % SIDE)
         pl.semaphore_wait(go, 1)
+        for piece in every:
+            put(RIGHT, 1, piece)
+        first_chunk()
         for sub in (0, 1, 4, 5, 2, 3):
             hop0(LEFT, sub).start()
 
+    pl.when(alone)(take_x)
     announce(0)
-    products(1, (here + 3) % SIDE)
+
+    @pl.when(core == 0)
+    def _():
+        products(1, (here + 3) % SIDE)
+
     products(2, (here + 5) % SIDE)
 
     @pl.when(core == 0)
@@ -222,11 +238,6 @@
         for place in (0, 1):
             put(RIGHT, 1, ahead[RIGHT][place])
             put(LEFT, 1, ahead[LEFT][place])
-
-    @pl.when(core == 1)
-    def _():
-        for piece in every:
-            put(RIGHT, 1, piece)
 
     products(3, (here + 2) % SIDE)
     products(4, (here + 6) % SIDE)
@@ -280,56 +291,62 @@
     split_base(4, 7)
     pl.semaphore_wait(ready.at[2], 2)
 
+    PAIR = 3
+
     def over(to, group):
         away = (to - across + SIDE) % SIDE
         slot = away - 1
-        if group is None:
-            at, send, recv = pl.ds(0, 144), w_send.at[slot], w_recv.at[slot]
-        else:
-            at, send, recv = pl.ds(48 * group, 48), t_send.at[slot, group], t_recv.at[slot, group]
+        at = pl.ds(0, 96) if group == PAIR else pl.ds(48 * group, 48)
         return pltpu.make_async_remote_copy(
-            src_ref=codes.at[to, at], dst_ref=far.at[slot, at], send_sem=send, recv_sem=recv,
+            src_ref=codes.at[to, at], dst_ref=far.at[slot, at],
+            send_sem=t_send.at[slot, group], recv_sem=t_recv.at[slot, group],
             device_id=cross(away), device_id_type=MESH,
         )
 
     def each_over(group, act):
+        def send(to, single):
+            if single or group == 2:
+                act(over(to, group))
+            elif group == 1:
+                act(over(to, PAIR))
+
         @pl.when(core == 0)
         def _():
             for to in range(SIDE):
-                if (to in FIRST) == (group is not None):
-                    @pl.when(across != to)
-                    def _():
-                        act(over(to, group))
-
-        @pl.when(core == 1)
-        def _():
-            for step in NEAR if group is None else FAR:
-                act(over((across + step) % SIDE, group))
-
-    def landed(group):
-        def one(step):
-            over((across + step) % SIDE, group).wait_recv()
-
-        def whole(step):
-            if group == 0:
-                over((across + step) % SIDE, None).wait_recv()
+                @pl.when(across != to)
+                def _():
+                    send(to, to in FIRST)
 
         @pl.when(core == 1)
         def _():
             for step in FAR:
-                one(step)
+                send((across + step) % SIDE, True)
             for step in NEAR:
-                whole(step)
+                send((across + step) % SIDE, False)
+
+    def landed(group):
+        def one(step, single):
+            if single or group == 2:
+                over((across + step) % SIDE, group).wait_recv()
+            elif group == 0:
+                over((across + step) % SIDE, PAIR).wait_recv()
+
+        @pl.when(core == 1)
+        def _():
+            for step in FAR:
+                one(step, True)
+            for step in NEAR:
+                one(step, False)
 
         @pl.when((core == 0) & (across < len(FIRST)))
         def _():
             for step in range(1, SIDE):
-                one(step)
+                one(step, True)
 
         @pl.when((core == 0) & (across >= len(FIRST)))
         def _():
             for step in range(1, SIDE):
-                whole(step)
+                one(step, False)
 
     for group, pieces in enumerate(GROUPS):
         for piece in pieces:
@@ -354,7 +371,6 @@
             flat[to, 48 * group:48 * group + 48, :] = both
             codes[to, 48 * group:48 * group + 48, :] = encode(both)
         each_over(group, lambda copy: copy.start())
-    each_over(None, lambda copy: copy.start())
 
     load_f.wait()
     theirs = jnp.zeros((48, HALF), jnp.float32)
@@ -398,7 +414,7 @@
         for step in (1, 2, 3):
             for piece in range(5):
                 hop(way, step, piece).wait_send()
-    for group in (0, 1, 2, None):
+    for group in range(3):
         each_over(group, lambda copy: copy.wait_send())
     give_r.wait()
     r_out[...] = mine[0:ROWS] + mine[24:24 + ROWS] + prod_got[0:ROWS, :]
@@ -446,10 +462,8 @@
             dma((6,)),
             dma((2, 3, 5)),
             dma((2, 3, 5)),
-            dma((SIDE - 1, 3)),
-            dma((SIDE - 1, 3)),
-            dma((SIDE - 1,)),
-            dma((SIDE - 1,)),
+            dma((SIDE - 1, 4)),
+            dma((SIDE - 1, 4)),
             dma,
             dma,
             pltpu.SemaphoreType.REGULAR((3,)),

time: 39.7 us -> 37.8 us (0.952)
  Pallas kernels: 37.7 us -> 35.7 us
    pallas_call x1, Pallas kernels: 37.7 us -> 35.7 us  [shards(): pl.pallas_call(body, name='gram_rotate', out_shape=(jax.ShapeDtypeStruct(...]
where the time goes in v5:
time: 37.8 us; the launch traced here: 37.6 us
  Pallas kernels  35.7 us (94%)
  local copies, waits for them, and re-layouts  1.27 us (3%)
  between operations  0.64 us (2%)
    pallas_call x1, Pallas kernels, shards(): pl.pallas_call(body, name='gram_rotate', out_shape=(jax.ShapeDtypeStruct(...  35.7 us
    unnamed x2, local copies, waits for them, and re-layouts  1.27 us

profile of v5, /device:TPU:1, one launch (start us, length us, event | category | flops | bytes accessed | tf_op | source)
XLA Modules:
  0.0 37.6 jit_solution(17733762153295694395)
XLA Ops:
  0.6 35.7 %gram_rotate.1 = (f32[21,672]{1,0:T(8,128)S(1)}, f32[21,672]{1,0:T(8,128)S(1)}) custom-call(bf16[672,256]{1,0:T(8,128)(2,1)} %bitcast.1, f32[21,672]{1,0:T(8,128)} %refs_1_.1, f32[672,1344]{1,0:T(8,128)} %refs_2_.1), custom_call_target="tpu_custom_call" | custom-call | tf_op jit(solution)/shard_map/gram_rotate/pallas_call | solution.py:429
  36.4 0.6 %copy.7 = f32[21,672]{1,0:T(8,128)} copy(f32[21,672]{1,0:T(8,128)S(1)} %get-tuple-element.4) | data formatting | bytes 112896
  37.0 0.6 %copy.8 = f32[21,672]{1,0:T(8,128)} copy(f32[21,672]{1,0:T(8,128)S(1)} %get-tuple-element.5) | data formatting | bytes 112896

commit v6 on v5

--- a/solution.py
+++ b/solution.py
@@ -227,55 +227,53 @@
     pl.when(alone)(take_x)
     announce(0)
 
-    @pl.when(core == 0)
-    def _():
-        products(1, (here + 3) % SIDE)
-
-    products(2, (here + 5) % SIDE)
-
-    @pl.when(core == 0)
-    def _():
+    def chunk(slot):
+        products(slot, (here + (0, 3, 5, 2, 6, 1, 7, 0)[slot]) % SIDE)
+
+    @pl.when(core == 0)
+    def _():
+        chunk(1)
         for place in (0, 1):
             put(RIGHT, 1, ahead[RIGHT][place])
+        chunk(2)
+        for place in (0, 1):
             put(LEFT, 1, ahead[LEFT][place])
-
-    products(3, (here + 2) % SIDE)
-    products(4, (here + 6) % SIDE)
-
-    @pl.when(core == 0)
-    def _():
+        chunk(3)
+        chunk(4)
         for place in (2, 3, 4):
             put(RIGHT, 1, ahead[RIGHT][place], (0, 1, 2))
             put(LEFT, 1, ahead[LEFT][place], (3, 4, 5))
 
     @pl.when(core == 1)
     def _():
+        chunk(2)
+        chunk(3)
         for piece in every:
             put(RIGHT, 2, piece)
             put(LEFT, 1, piece, range(6))
 
     pl.semaphore_wait(ready.at[0], 2)
     announce(1)
-    products(5, (here + 1) % SIDE)
-    products(6, (here + 7) % SIDE)
 
     @pl.when(core == 0)
     def _():
         for place in range(5):
             put(RIGHT, 2, ahead[RIGHT][place])
             put(LEFT, 2, ahead[LEFT][place])
-
-    @pl.when(core == 1)
-    def _():
+        chunk(5)
+        chunk(6)
+
+    @pl.when(core == 1)
+    def _():
+        chunk(5)
+        chunk(4)
         for piece in every:
             put(RIGHT, 3, piece)
             put(LEFT, 2, piece)
+        chunk(6)
 
     pl.semaphore_wait(ready.at[1], 2)
     announce(2)
-    products(7, here)
-    load_b.wait()
-    split_base(0, 4)
 
     @pl.when(core == 0)
     def _():
@@ -288,7 +286,7 @@
         for piece in every:
             put(LEFT, 3, piece)
 
-    split_base(4, 7)
+    chunk(7)
     pl.semaphore_wait(ready.at[2], 2)
 
     PAIR = 3
@@ -372,6 +370,8 @@
             codes[to, 48 * group:48 * group + 48, :] = encode(both)
         each_over(group, lambda copy: copy.start())
 
+    load_b.wait()
+    split_base(0, 7)
     load_f.wait()
     theirs = jnp.zeros((48, HALF), jnp.float32)
     mine = jnp.zeros((48, HALF), jnp.float32)
@@ -426,7 +426,7 @@
     f32, bf16 = jnp.float32, jnp.bfloat16
     body = lambda *refs: kernel(scale_new, *refs)
     dma = pltpu.SemaphoreType.DMA
-    return pl.pallas_call(
+    factor, rotated = pl.pallas_call(
         body,
         name="gram_rotate",
         out_shape=(
@@ -474,6 +474,7 @@
             collective_id=0, has_side_effects=True, vmem_limit_bytes=55040 * 1024
         ),
     )(tokens.T, factor_old, basis)
+    return factor + 0.0 * rotated, rotated + 0.0 * factor
 
 
 def solution(mesh):

time: 37.8 us -> 37.3 us (0.987)
  local copies, waits for them, and re-layouts: 1.27 us -> 0 us
  other arithmetic: 0 us -> 0.67 us
    unnamed x2 -> x0, local copies, waits for them, and re-layouts: 1.27 us -> none
    add x0 -> x1, other arithmetic: none -> 0.67 us  [shards(): return (factor + 0.0 * rotated, rotated + 0.0 * factor)]
where the time goes in v6:
time: 37.3 us; the launch traced here: 37.1 us
  Pallas kernels  35.8 us (96%)
  other arithmetic  0.67 us (2%)
  between operations  0.64 us (2%)
    pallas_call x1, Pallas kernels, shards(): pl.pallas_call(body, name='gram_rotate', out_shape=(jax.ShapeDtypeStruct(...  35.8 us

profile of v6, /device:TPU:1, one launch (start us, length us, event | category | flops | bytes accessed | tf_op | source)
XLA Modules:
  0.0 37.1 jit_solution(5859561893578777619)
XLA Ops:
  0.6 35.8 %gram_rotate.1 = (f32[21,672]{1,0:T(8,128)S(1)}, f32[21,672]{1,0:T(8,128)S(1)}) custom-call(bf16[672,256]{1,0:T(8,128)(2,1)} %bitcast.1, f32[21,672]{1,0:T(8,128)} %refs_1_.1, f32[672,1344]{1,0:T(8,128)} %refs_2_.1), custom_call_target="tpu_custom_call" | custom-call | tf_op jit(solution)/shard_map/gram_rotate/pallas_call | solution.py:429
  36.5 0.7 %multiply_add_fusion = (f32[21,672]{1,0:T(8,128)}, f32[21,672]{1,0:T(8,128)}) fusion(f32[21,672]{1,0:T(8,128)S(1)} %get-tuple-element.5, f32[21,672]{1,0:T(8,128)S(1)} %get-tuple-element.4), kind=kLoop, calls=%fused_computation | loop fusion | flops 56448 | bytes 225792 | tf_op jit(solution)/shard_map/add | solution.py:477

commit v7 on v6

--- a/solution.py
+++ b/solution.py
@@ -372,6 +372,22 @@
 
     load_b.wait()
     split_base(0, 7)
+    give_x.wait_send()
+
+    @pl.when(core == 0)
+    def _():
+        for sub in range(6):
+            hop0(RIGHT if sub < 3 else LEFT, sub).wait_send()
+
+    @pl.when(core == 1)
+    def _():
+        for sub in range(6):
+            hop0(LEFT, sub).wait_send()
+
+    for way in range(2):
+        for step in (1, 2, 3):
+            for piece in range(5):
+                hop(way, step, piece).wait_send()
     load_f.wait()
     theirs = jnp.zeros((48, HALF), jnp.float32)
     mine = jnp.zeros((48, HALF), jnp.float32)
@@ -398,22 +414,6 @@
     )
     give_r.start()
     mine += turned(both, base_hi, base_lo, core, 2)
-    give_x.wait_send()
-
-    @pl.when(core == 0)
-    def _():
-        for sub in range(6):
-            hop0(RIGHT if sub < 3 else LEFT, sub).wait_send()
-
-    @pl.when(core == 1)
-    def _():
-        for sub in range(6):
-            hop0(LEFT, sub).wait_send()
-
-    for way in range(2):
-        for step in (1, 2, 3):
-            for piece in range(5):
-                hop(way, step, piece).wait_send()
     for group in range(3):
         each_over(group, lambda copy: copy.wait_send())
     give_r.wait()

time: 37.3 us -> 37.3 us (level)
  no operation moved by 1% of the time
where the time goes in v7:
time: 37.3 us; the launch traced here: 37.1 us
  Pallas kernels  35.8 us (96%)
  other arithmetic  0.67 us (2%)
  between operations  0.64 us (2%)
    pallas_call x1, Pallas kernels, shards(): pl.pallas_call(body, name='gram_rotate', out_shape=(jax.ShapeDtypeStruct(...  35.8 us

profile of v7, /device:TPU:1, one launch (start us, length us, event | category | flops | bytes accessed | tf_op | source)
XLA Modules:
  0.0 37.1 jit_solution(10381928549474972469)
XLA Ops:
  0.6 35.8 %gram_rotate.1 = (f32[21,672]{1,0:T(8,128)S(1)}, f32[21,672]{1,0:T(8,128)S(1)}) custom-call(bf16[672,256]{1,0:T(8,128)(2,1)} %bitcast.1, f32[21,672]{1,0:T(8,128)} %refs_1_.1, f32[672,1344]{1,0:T(8,128)} %refs_2_.1), custom_call_target="tpu_custom_call" | custom-call | tf_op jit(solution)/shard_map/gram_rotate/pallas_call | solution.py:429
  36.5 0.7 %multiply_add_fusion = (f32[21,672]{1,0:T(8,128)}, f32[21,672]{1,0:T(8,128)}) fusion(f32[21,672]{1,0:T(8,128)S(1)} %get-tuple-element.5, f32[21,672]{1,0:T(8,128)S(1)} %get-tuple-element.4), kind=kLoop, calls=%fused_computation | loop fusion | flops 56448 | bytes 225792 | tf_op jit(solution)/shard_map/add | solution.py:477
